TPU v7x, 256 devices: a whole 4x4x8 slice. The times are simulated.
256 devices in a mesh: batch: 4 (over y), expert: 64 (over x, z, core).
Axes of the slice: x: 4, y: 4, z: 8, core: 2. Of those that a mesh axis runs over, the one named last changes fastest.
Arguments:
- tokens: bfloat16 [32768, 1024], P(('batch', 'expert')), may hold values from -6 to 6
- cotangent: bfloat16 [32768, 1024], P(('batch', 'expert')), may hold values from -6 to 6
- domain_ids: int32 [32768], P(('batch', 'expert')), may hold values from 0 to 7
- shared_ids: int32 [32768, 2], P(('batch', 'expert')), may hold values from 0 to 63, all different within a row
- private_ids: int32 [32768, 2], P(('batch', 'expert')), may hold values from 0 to 7, all different within a row
- gate_weight: bfloat16 [1024, 8, 72], replicated, may hold values from -0.375 to 0.375
- shared_in: bfloat16 [64, 1024, 2048], P('expert', None, 'batch'), may hold values from -0.1875 to 0.1875
- shared_out: bfloat16 [64, 2048, 1024], P('expert', 'batch'), may hold values from -0.125 to 0.125
- private_in: bfloat16 [64, 1024, 2048], P('expert', None, 'batch'), may hold values from -0.1875 to 0.1875
- private_out: bfloat16 [64, 2048, 1024], P('expert', 'batch'), may hold values from -0.125 to 0.125
Outputs:
- mixed: bfloat16 [32768, 1024], P(('batch', 'expert'))
- grad_shared_in: bfloat16 [64, 1024, 2048], P('expert', None, 'batch')
- grad_shared_out: bfloat16 [64, 2048, 1024], P('expert', 'batch')
- grad_private_in: bfloat16 [64, 1024, 2048], P('expert', None, 'batch')
- grad_private_out: bfloat16 [64, 2048, 1024], P('expert', 'batch')
- grad_gate: float32 [1024, 8, 72], P(('batch', 'expert'))
All inputs are finite; a program needn't handle non-finite values.
Results may differ from a plain program's by a relative error of at most 0.015.
Values may be sent and summed in bfloat16 or wider, within the bound.
No kernel may reach another device: no remote copies, remote signals or barrier semaphores. Data moves between devices by JAX's collectives and lax.ppermute only.
A program may use at most 128 MiB of HBM per device.

v0:
```python
import jax
import jax.numpy as jnp
from jax import lax
from jax.sharding import PartitionSpec as P

SHARED = 64
PRIV = 8
DOMAINS = 8
PRIVATE = 64
GATES = 72
CAP = 4


def silu_slope(values):
    sigmoid = jax.nn.sigmoid(values)
    return sigmoid * (1.0 + values * (1.0 - sigmoid))


def routing(expert_ids, number, height):
    experts = jnp.arange(number, dtype=jnp.int32)
    onehot = (expert_ids[:, :, None] == experts[None, None, :]).astype(jnp.float32)
    per_row = jnp.sum(onehot, axis=1)
    order = jnp.arange(height, dtype=jnp.int32)
    lower = (order[:, None] > order[None, :]).astype(jnp.bfloat16)
    earlier = jnp.dot(lower, per_row.astype(jnp.bfloat16), preferred_element_type=jnp.float32)
    slots = jnp.sum(onehot * earlier[:, None, :], axis=2).astype(jnp.int32)
    target = jnp.where(slots < CAP, expert_ids * CAP + slots, -1)
    cells = jnp.arange(number * CAP, dtype=jnp.int32)
    return [
        (cells[:, None] == target[None, :, pick_index]).astype(jnp.float32)
        for pick_index in range(2)
    ]


def pack_rows(selectors, tokens, features):
    placed = (selectors[0] + selectors[1]).astype(jnp.bfloat16)
    packed = jnp.dot(placed, tokens, preferred_element_type=jnp.float32)
    return packed.astype(jnp.bfloat16).reshape(-1, CAP, features)


def pack_scaled(selectors, gate_pair, cot_float, features):
    weighted = selectors[0] * gate_pair[None, :, 0] + selectors[1] * gate_pair[None, :, 1]
    packed = jnp.dot(weighted, cot_float, precision=lax.Precision.HIGHEST)
    return packed.astype(jnp.bfloat16).reshape(-1, CAP, features)


def unpack_rows(selector, returned, features):
    flat = returned.reshape(-1, features)
    return jnp.dot(selector.T.astype(jnp.bfloat16), flat, preferred_element_type=jnp.float32)


def forward_experts(inputs_x, weight_a, weight_b):
    pre = jnp.einsum("erd,edh->erh", inputs_x, weight_a, preferred_element_type=jnp.float32)
    act = jax.nn.silu(pre).astype(jnp.bfloat16)
    outputs = jnp.einsum("erh,ehd->erd", act, weight_b, preferred_element_type=jnp.float32)
    return (pre, act, outputs)


def backward_experts(pre, scaled, weight_b):
    slope = jnp.einsum("erd,ehd->erh", scaled, weight_b, preferred_element_type=jnp.float32)
    return (slope * silu_slope(pre)).astype(jnp.bfloat16)


def body(
    tokens,
    cotangent,
    domain_ids,
    shared_ids,
    private_ids,
    gate_weight,
    shared_in,
    shared_out,
    private_in,
    private_out,
):
    height, features = tokens.shape
    columns_all = DOMAINS * GATES
    table = jnp.dot(
        tokens, gate_weight.reshape(features, columns_all), preferred_element_type=jnp.float32
    )
    base = domain_ids[:, None] * GATES
    columns = jnp.concatenate([base + shared_ids, base + SHARED + private_ids], axis=1)
    picked = (
        columns[:, :, None] == jnp.arange(columns_all, dtype=jnp.int32)[None, None, :]
    ).astype(jnp.float32)
    logits = jnp.sum(table[:, None, :] * picked, axis=2)
    gates = jax.nn.softmax(logits, axis=1)
    shared_sel = routing(shared_ids, SHARED, height)
    private_sel = routing(domain_ids[:, None] * PRIV + private_ids, PRIVATE, height)
    send_shared = pack_rows(shared_sel, tokens, features)
    send_private = pack_rows(private_sel, tokens, features)
    cot_float = cotangent.astype(jnp.float32)
    scaled_shared = pack_scaled(shared_sel, gates[:, 0:2], cot_float, features)
    scaled_private = pack_scaled(private_sel, gates[:, 2:4], cot_float, features)
    got_shared, got_private = (
        lax.all_to_all(send_shared, "expert", split_axis=0, concat_axis=1, tiled=True),
        lax.all_to_all(send_private, "expert", split_axis=0, concat_axis=1, tiled=True),
    )
    full_shared_in, full_shared_out, full_private_in, full_private_out = (
        lax.all_gather(shared_in, "batch", axis=2, tiled=True),
        lax.all_gather(shared_out, "batch", axis=1, tiled=True),
        lax.all_gather(private_in, "batch", axis=2, tiled=True),
        lax.all_gather(private_out, "batch", axis=1, tiled=True),
    )
    pre_shared, act_shared, out_shared = forward_experts(
        got_shared, full_shared_in, full_shared_out
    )
    pre_private, act_private, out_private = forward_experts(
        got_private, full_private_in, full_private_out
    )
    back_shared, back_private = (
        lax.all_to_all(
            out_shared.astype(jnp.bfloat16), "expert", split_axis=1, concat_axis=0, tiled=True
        ),
        lax.all_to_all(
            out_private.astype(jnp.bfloat16), "expert", split_axis=1, concat_axis=0, tiled=True
        ),
    )
    pick_outputs = [unpack_rows(selector, back_shared, features) for selector in shared_sel]
    pick_outputs = pick_outputs + [
        unpack_rows(selector, back_private, features) for selector in private_sel
    ]
    mixed = gates[:, 0:1] * pick_outputs[0] + gates[:, 1:2] * pick_outputs[1]
    mixed = mixed + gates[:, 2:3] * pick_outputs[2] + gates[:, 3:4] * pick_outputs[3]
    dgate = jnp.stack(
        [jnp.sum(cot_float * output_rows, axis=1) for output_rows in pick_outputs], axis=1
    )
    dlogit = gates * (dgate - jnp.sum(gates * dgate, axis=1, keepdims=True))
    spread = jnp.sum(dlogit[:, :, None] * picked, axis=1)
    gate_term = jnp.dot(
        tokens.astype(jnp.float32).T, spread, precision=lax.Precision.HIGHEST
    ).reshape(features, DOMAINS, GATES)
    grad_gate = lax.psum_scatter(gate_term, ("batch", "expert"), scatter_dimension=0, tiled=True)
    got_gshared, got_gprivate = (
        lax.all_to_all(scaled_shared, "expert", split_axis=0, concat_axis=1, tiled=True),
        lax.all_to_all(scaled_private, "expert", split_axis=0, concat_axis=1, tiled=True),
    )
    back_grad_shared = backward_experts(pre_shared, got_gshared, full_shared_out)
    back_grad_private = backward_experts(pre_private, got_gprivate, full_private_out)
    term_shared_out = jnp.einsum(
        "erh,erd->ehd", act_shared, got_gshared, preferred_element_type=jnp.float32
    )
    term_shared_in = jnp.einsum(
        "erd,erh->edh", got_shared, back_grad_shared, preferred_element_type=jnp.float32
    )
    term_private_out = jnp.einsum(
        "erh,erd->ehd", act_private, got_gprivate, preferred_element_type=jnp.float32
    )
    term_private_in = jnp.einsum(
        "erd,erh->edh", got_private, back_grad_private, preferred_element_type=jnp.float32
    )
    summed = (
        lax.psum_scatter(
            term_shared_in.astype(jnp.bfloat16), "batch", scatter_dimension=2, tiled=True
        ).astype(jnp.float32),
        lax.psum_scatter(
            term_shared_out.astype(jnp.bfloat16), "batch", scatter_dimension=1, tiled=True
        ).astype(jnp.float32),
        lax.psum_scatter(
            term_private_in.astype(jnp.bfloat16), "batch", scatter_dimension=2, tiled=True
        ).astype(jnp.float32),
        lax.psum_scatter(
            term_private_out.astype(jnp.bfloat16), "batch", scatter_dimension=1, tiled=True
        ).astype(jnp.float32),
    )
    grad_shared_in = summed[0].astype(jnp.bfloat16)
    grad_shared_out = summed[1].astype(jnp.bfloat16)
    grad_private_in = summed[2].astype(jnp.bfloat16)
    grad_private_out = summed[3].astype(jnp.bfloat16)
    return (
        mixed.astype(jnp.bfloat16),
        grad_shared_in,
        grad_shared_out,
        grad_private_in,
        grad_private_out,
        grad_gate,
    )


def solution(mesh):
    return jax.shard_map(
        body,
        mesh=mesh,
        in_specs=(
            P(("batch", "expert"), None),
            P(("batch", "expert"), None),
            P(("batch", "expert")),
            P(("batch", "expert"), None),
            P(("batch", "expert"), None),
            P(),
            P("expert", None, "batch"),
            P("expert", "batch", None),
            P("expert", None, "batch"),
            P("expert", "batch", None),
        ),
        out_specs=(
            P(("batch", "expert"), None),
            P("expert", None, "batch"),
            P("expert", "batch", None),
            P("expert", None, "batch"),
            P("expert", "batch", None),
            P(("batch", "expert"), None, None),
        ),
        check_vma=False,
    )
```

profile of v0, /device:TPU:1, one launch (start us, length us, event | category | flops | bytes accessed | tf_op | source)
XLA Modules:
  0.0 1748.5 jit_solution(1115050402414843876)
XLA Ops:
  7.3 0.7 all-gather.9.cloned.1.call-update
  8.0 0.7 all-gather.11.cloned.1.call-update
  8.8 0.7 all-gather.5.cloned.1.call-update
  9.5 0.5 all-gather.7.cloned.1.call-update
  10.1 0.1 fusion.81
  10.3 0.6 broadcast_add_fusion.1
  10.9 0.1 fusion.80
  11.1 0.3 convolution_convert_fusion.2
  11.4 1.0 reshape.256
  12.3 13.0 all-to-all-start.2
  25.4 0.3 convolution_convert_fusion.3
  25.6 1.0 reshape.251
  26.6 16.0 all-to-all-done.2
  42.7 6.3 all-to-all-start
  49.1 17.2 all-to-all-done
  66.4 4.9 fusion.4
  71.4 46.2 %all-gather.11.cloned.1.call-done = bf16[1,2048,1024]{2,1,0:T(8,128)(2,1)} async-done(((bf16[1,512,1024]{2,1,0:T(8,128)(2,1)}), bf16[1,2048,1024]{2,1,0:T(8,128)(2,1)}) %all-gather.11.cloned.1.call-update) | async-done | bytes 4194320 | tf_op jit(solution)/shard_map/all_gather | solution.py:103
  117.6 4.1 fusion.30
  121.7 0.8 copy.69
  122.5 0.5 broadcast.105
  123.0 3.7 reduce
  126.7 1.1 reshape.266
  127.8 10.7 all-to-all-start.3
  138.5 32.1 %all-gather.5.cloned.1.call-done = bf16[1,1024,2048]{2,1,0:T(8,128)(2,1)} async-done(((bf16[1,1024,512]{2,1,0:T(8,128)(2,1)}), bf16[1,1024,2048]{2,1,0:T(8,128)(2,1)}) %all-gather.5.cloned.1.call-update) | async-done | bytes 4194320 | tf_op jit(solution)/shard_map/all_gather | solution.py:100
  170.6 4.8 fusion.10
  175.4 48.1 %all-gather.7.cloned.1.call-done = bf16[1,2048,1024]{2,1,0:T(8,128)(2,1)} async-done(((bf16[1,512,1024]{2,1,0:T(8,128)(2,1)}), bf16[1,2048,1024]{2,1,0:T(8,128)(2,1)}) %all-gather.7.cloned.1.call-update) | async-done | bytes 4194320 | tf_op jit(solution)/shard_map/all_gather | solution.py:101
  223.5 4.1 fusion.33
  227.6 0.8 copy.70
  228.4 3.7 reduce.1
  232.1 1.1 reshape.268
  233.3 10.7 all-to-all-start.1
  244.0 0.7 pad_add_fusion
  244.7 0.5 fusion.91
  245.2 0.1 select_reduce_fusion.1
  245.4 0.5 reshape.267
  245.9 0.3 fusion.44
  246.2 0.3 fusion.46
  246.6 14.7 all-to-all-done.1
  261.3 0.5 reshape.269
  261.8 0.3 fusion.48
  262.2 1.2 fusion.40
  263.4 0.1 select_reduce_fusion
  263.5 1.1 fusion.92
  264.6 3.5 copy.46
  268.1 0.3 reduce-scatter.6.cloned.1.call-start
  268.4 0.6 copy-done.7
  269.0 0.6 convolution_convert_fusion.1
  269.6 0.2 reshape.261
  269.8 24.2 %all_to_all.24 = bf16[64,4,1024]{2,1,0:T(4,128)(2,1)S(1)} all-to-all(bf16[64,4,1024]{2,1,0:T(4,128)(2,1)S(1)} %reshape.261), channel_id=1, replica_groups=mesh['batch'=4,'expert'=64] {'expert'}, dimensions={0} | all-to-all | bytes 1048576 | tf_op jit(solution)/shard_map/all_to_all | solution.py:135
  294.1 7.4 convert_bitcast_fusion.3
  301.6 4.9 convert_bitcast_fusion.2
  306.7 0.6 convolution_convert_fusion
  307.2 0.2 reshape.263
  307.4 23.3 %all_to_all.25 = bf16[64,4,1024]{2,1,0:T(4,128)(2,1)S(1)} all-to-all(bf16[64,4,1024]{2,1,0:T(4,128)(2,1)S(1)} %reshape.263), channel_id=1, replica_groups=mesh['batch'=4,'expert'=64] {'expert'}, dimensions={0} | all-to-all | bytes 1048576 | tf_op jit(solution)/shard_map/all_to_all | solution.py:136
  330.9 7.4 convert_bitcast_fusion.1
  338.4 4.9 convert_bitcast_fusion
  343.3 1.0 copy-done.3
  344.3 0.2 copy-done.8
  344.5 0.9 add_convert_fusion
  345.4 1189.0 %reduce-scatter.14.cloned.1.call-done = f32[4,8,72]{2,1,0:T(8,128)} async-done(((f32[1024,8,72]{2,1,0:T(8,128)}), f32[4,8,72]{2,1,0:T(8,128)}) %reduce-scatter.14.cloned.1.call-update) | async-done | bytes 9232 | tf_op jit(solution)/shard_map/reduce_scatter | solution.py:133
  1534.4 50.5 %reduce-scatter.6.cloned.1.call-done = bf16[1,1024,512]{2,1,0:T(8,128)(2,1)} async-done(((bf16[1,1024,2048]{2,1,0:T(8,128)(2,1)}), bf16[1,1024,512]{2,1,0:T(8,128)(2,1)}) %reduce-scatter.6.cloned.1.call-update) | async-done | bytes 1048592 | tf_op jit(solution)/shard_map/reduce_scatter | solution.py:153
  1584.9 52.3 %reduce-scatter.8.cloned.1.call-done = bf16[1,512,1024]{2,1,0:T(8,128)(2,1)} async-done(((bf16[1,2048,1024]{2,1,0:T(8,128)(2,1)}), bf16[1,512,1024]{2,1,0:T(8,128)(2,1)}) %reduce-scatter.8.cloned.1.call-update) | async-done | bytes 1048592 | tf_op jit(solution)/shard_map/reduce_scatter | solution.py:156
  1637.2 52.4 %reduce-scatter.10.cloned.1.call-done = bf16[1,1024,512]{2,1,0:T(8,128)(2,1)} async-done(((bf16[1,1024,2048]{2,1,0:T(8,128)(2,1)}), bf16[1,1024,512]{2,1,0:T(8,128)(2,1)}) %reduce-scatter.10.cloned.1.call-update) | async-done | bytes 1048592 | tf_op jit(solution)/shard_map/reduce_scatter | solution.py:159
  1689.6 52.3 %reduce-scatter.12.cloned.1.call-done = bf16[1,512,1024]{2,1,0:T(8,128)(2,1)} async-done(((bf16[1,2048,1024]{2,1,0:T(8,128)(2,1)}), bf16[1,512,1024]{2,1,0:T(8,128)(2,1)}) %reduce-scatter.12.cloned.1.call-update) | async-done | bytes 1048592 | tf_op jit(solution)/shard_map/reduce_scatter | solution.py:162
  (61 shorter events, 1.2 us)
Async XLA Ops:
  7.2 237.5 %copy-start = (bf16[1024,8,72]{0,2,1:T(8,128)(2,1)S(1)}, bf16[1024,8,72]{0,2,1:T(8,128)(2,1)}, u32[]{:S(2)}) copy-start(bf16[1024,8,72]{0,2,1:T(8,128)(2,1)} %param.15) | copy-start | bytes 3538948
  7.2 2.8 copy-start.13
  7.2 3.0 copy-start.15
  7.2 3.1 copy-start.14
  7.2 3.8 copy-start.4
  7.2 59.2 %all-gather.9.cloned.1.call-start = ((), (), s32[]{:S(2)}) async-start(), calls=%async_computation.13 | async-start | bytes 5242880 | tf_op jit(solution)/shard_map/all_gather | solution.py:102
  8.0 109.6 %all-gather.11.cloned.1.call-start = ((), (), s32[]{:S(2)}) async-start(), calls=%async_computation.14 | async-start | bytes 5242880 | tf_op jit(solution)/shard_map/all_gather | solution.py:103
  8.7 161.9 %all-gather.5.cloned.1.call-start = ((), (), s32[]{:S(2)}) async-start(), calls=%async_computation.11 | async-start | bytes 5242880 | tf_op jit(solution)/shard_map/all_gather | solution.py:100
  9.4 214.1 %all-gather.7.cloned.1.call-start = ((), (), s32[]{:S(2)}) async-start(), calls=%async_computation.12 | async-start | bytes 5242880 | tf_op jit(solution)/shard_map/all_gather | solution.py:101
  12.3 30.3 %all-to-all-start.2 = ((bf16[64,4,1024]{2,1,0:T(4,128)(2,1)}), bf16[64,4,1024]{2,1,0:T(4,128)(2,1)S(1)}, u32[]{:S(2)}, u32[]{:S(2)}) async-start(bf16[64,4,1024]{2,1,0:T(4,128)(2,1)} %reshape.256), calls=%async_computation.2 | async-start | bytes 1048576 | tf_op jit(solution)/shard_map/all_to_all | solution.py:97
  42.7 23.6 %all-to-all-start = ((bf16[64,4,1024]{2,1,0:T(4,128)(2,1)}), bf16[64,4,1024]{2,1,0:T(4,128)(2,1)S(1)}, u32[]{:S(2)}, u32[]{:S(2)}) async-start(bf16[64,4,1024]{2,1,0:T(4,128)(2,1)} %reshape.251), calls=%async_computation | async-start | bytes 1048576 | tf_op jit(solution)/shard_map/all_to_all | solution.py:96
  49.1 22.3 %copy-start.9 = (bf16[256,1024]{1,0:T(8,128)(2,1)}, bf16[256,1024]{1,0:T(8,128)(2,1)S(1)}, u32[]{:S(2)}) copy-start(bf16[256,1024]{1,0:T(8,128)(2,1)S(1)} %reshape.257) | copy-start | bytes 1572868
  66.4 104.2 %copy-start.11 = (bf16[256,1024]{1,0:T(8,128)(2,1)}, bf16[256,1024]{1,0:T(8,128)(2,1)S(1)}, u32[]{:S(2)}) copy-start(bf16[256,1024]{1,0:T(8,128)(2,1)S(1)} %reshape.252) | copy-start | bytes 1572868
  127.8 105.4 %all-to-all-start.3 = ((bf16[64,2,2048]{2,1,0:T(2,128)(2,1)}), bf16[64,2,2048]{2,1,0:T(2,128)(2,1)S(1)}, u32[]{:S(2)}, u32[]{:S(2)}) async-start(bf16[64,2,2048]{2,1,0:T(2,128)(2,1)} %reshape.266), calls=%async_computation.3 | async-start | bytes 1048576 | tf_op jit(solution)/shard_map/all_to_all | solution.py:115
  233.3 28.0 %all-to-all-start.1 = ((bf16[64,2,2048]{2,1,0:T(2,128)(2,1)}), bf16[64,2,2048]{2,1,0:T(2,128)(2,1)S(1)}, u32[]{:S(2)}, u32[]{:S(2)}) async-start(bf16[64,2,2048]{2,1,0:T(2,128)(2,1)} %reshape.268), calls=%async_computation.1 | async-start | bytes 1048576 | tf_op jit(solution)/shard_map/all_to_all | solution.py:112
  243.9 1290.4 %reduce-scatter.14.cloned.1.call-start = ((), (), s32[]{:S(2)}) async-start(), calls=%async_computation.19 | async-start | bytes 4210688 | tf_op jit(solution)/shard_map/reduce_scatter | solution.py:133
  246.2 15.9 copy-start.6
  261.8 1.7 copy-start.5
  262.1 2.5 copy-start.2
  268.1 0.9 copy-start.7
  268.1 26.0 %copy-start.12 = (bf16[256,1024]{1,0:T(8,128)(2,1)S(1)}, bf16[256,1024]{1,0:T(8,128)(2,1)}, u32[]{:S(2)}) copy-start(bf16[256,1024]{1,0:T(8,128)(2,1)} %copy-done.11) | copy-start | bytes 1572868
  268.1 1316.8 %reduce-scatter.6.cloned.1.call-start = ((), (), s32[]{:S(2)}) async-start(), calls=%async_computation.15 | async-start | bytes 5242880 | tf_op jit(solution)/shard_map/reduce_scatter | solution.py:153
  301.6 1335.6 %reduce-scatter.8.cloned.1.call-start = ((), (), s32[]{:S(2)}) async-start(), calls=%async_computation.16 | async-start | bytes 5242880 | tf_op jit(solution)/shard_map/reduce_scatter | solution.py:156
  306.6 24.3 %copy-start.10 = (bf16[256,1024]{1,0:T(8,128)(2,1)S(1)}, bf16[256,1024]{1,0:T(8,128)(2,1)}, u32[]{:S(2)}) copy-start(bf16[256,1024]{1,0:T(8,128)(2,1)} %copy-done.9) | copy-start | bytes 1572868
  306.6 1383.0 %reduce-scatter.10.cloned.1.call-start = ((), (), s32[]{:S(2)}) async-start(), calls=%async_computation.17 | async-start | bytes 5242880 | tf_op jit(solution)/shard_map/reduce_scatter | solution.py:159
  338.3 1403.6 %reduce-scatter.12.cloned.1.call-start = ((), (), s32[]{:S(2)}) async-start(), calls=%async_computation.18 | async-start | bytes 5242880 | tf_op jit(solution)/shard_map/reduce_scatter | solution.py:162
  343.3 1.0 copy-start.3
  343.3 1.2 copy-start.8
  343.3 1398.6 %copy-start.1 = (bf16[1024,8,72]{0,2,1:T(8,128)(2,1)S(1)}, bf16[1024,8,72]{0,2,1:T(8,128)(2,1)}, u32[]{:S(2)}) copy-start(bf16[1024,8,72]{0,2,1:T(8,128)(2,1)} %param.15) | copy-start | bytes 3538948
Sparse Core Ops, SparseCore 0:
  9.9 54.5 all-gather.8
  66.3 51.2 all-gather.10
  119.4 51.1 all-gather.4
  172.2 51.2 all-gather.6
  268.2 1266.0 reduce-scatter.13
  1537.5 47.3 reduce-scatter.5
  1588.0 49.1 reduce-scatter.7
  1640.5 49.1 reduce-scatter.9
  1692.8 49.1 reduce-scatter.11
where the time goes:
time: 1750 us
  waiting for transfers between devices  1570 us (90%)
  matrix products  48.2 us (3%)
  blocking collectives  47.5 us (3%)
  starting transfers between devices  41.2 us (2%)
    reduce_scatter x1, waiting for transfers between devices, body(): lax.psum_scatter(gate_term, ('batch', 'expert'), scatter_dimension=0, til...  1190 us
    reduce_scatter x1, waiting for transfers between devices, body(): lax.psum_scatter(term_private_in.astype(jnp.bfloat16), 'batch', scatter_d...  52.4 us
    reduce_scatter x1, waiting for transfers between devices, body(): lax.psum_scatter(term_private_out.astype(jnp.bfloat16), 'batch', scatter_...  52.3 us
    reduce_scatter x1, waiting for transfers between devices, body(): lax.psum_scatter(term_shared_out.astype(jnp.bfloat16), 'batch', scatter_d...  52.3 us
    reduce_scatter x1, waiting for transfers between devices, body(): lax.psum_scatter(term_shared_in.astype(jnp.bfloat16), 'batch', scatter_di...  50.5 us
    all_gather x1, waiting for transfers between devices, body(): lax.all_gather(shared_out, 'batch', axis=1, tiled=True)  48.1 us
    all_gather x1, waiting for transfers between devices, body(): lax.all_gather(private_out, 'batch', axis=1, tiled=True)  46.2 us
  transfers between devices with their start and end apart: 13, of which 11 were waited for; matrix products, arithmetic and copies ran while one was open for 4% of the time, Pallas kernels for 0%

commit v1 on v0

--- a/solution.py
+++ b/solution.py
@@ -9,6 +9,24 @@
 PRIVATE = 64
 GATES = 72
 CAP = 4
+
+
+def ring_gather(shard, axis, dim):
+    ways, here, step = (lax.axis_size(axis), lax.axis_index(axis), shard.shape[dim])
+    dims = [n * ways if d == dim else n for d, n in enumerate(shard.shape)]
+    full = lax.dynamic_update_slice_in_dim(
+        jnp.zeros(dims, shard.dtype), shard, here * step, axis=dim
+    )
+    going_up = going_down = shard
+    for far in range(1, ways // 2 + 1):
+        going_up = lax.ppermute(going_up, axis, [(d, (d + 1) % ways) for d in range(ways)])
+        full = lax.dynamic_update_slice_in_dim(full, going_up, (here - far) % ways * step, axis=dim)
+        if 2 * far < ways:
+            going_down = lax.ppermute(going_down, axis, [(d, (d - 1) % ways) for d in range(ways)])
+            full = lax.dynamic_update_slice_in_dim(
+                full, going_down, (here + far) % ways * step, axis=dim
+            )
+    return full
 
 
 def silu_slope(values):
@@ -98,7 +116,7 @@
     )
     full_shared_in, full_shared_out, full_private_in, full_private_out = (
         lax.all_gather(shared_in, "batch", axis=2, tiled=True),
-        lax.all_gather(shared_out, "batch", axis=1, tiled=True),
+        ring_gather(shared_out, "batch", 1),
         lax.all_gather(private_in, "batch", axis=2, tiled=True),
         lax.all_gather(private_out, "batch", axis=1, tiled=True),
     )

time: 1750 us -> 1730 us (0.989)
  waiting for transfers between devices: 1570 us -> 1540 us
    all_gather x1 -> x0, waiting for transfers between devices: 48.1 us -> none  [body(): lax.all_gather(shared_out, 'batch', axis=1, tiled=True)]
    ppermute x0 -> x3, waiting for transfers between devices: none -> 43.2 us  [the longest x2 36 us: ring_gather(): lax.ppermute(going_up, axis, [(d, (d + 1) % ways) for d in range(ways)])]
  transfers between devices with their start and end apart: 13 -> 15, of which waited for: 11 -> 12; matrix products, arithmetic and copies ran while one was open for 4% -> 4% of each run, Pallas kernels for 0% -> 0%
where the time goes in v1:
time: 1730 us
  waiting for transfers between devices  1540 us (89%)
  starting transfers between devices  47.7 us (3%)
  blocking collectives  47.3 us (3%)
  matrix products  47.2 us (3%)
  local copies, waits for them, and re-layouts  25.8 us (1%)
    reduce_scatter x1, waiting for transfers between devices, body(): lax.psum_scatter(gate_term, ('batch', 'expert'), scatter_dimension=0, til...  1190 us
    reduce_scatter x1, waiting for transfers between devices, body(): lax.psum_scatter(term_private_in.astype(jnp.bfloat16), 'batch', scatter_d...  52.4 us
    reduce_scatter x1, waiting for transfers between devices, body(): lax.psum_scatter(term_private_out.astype(jnp.bfloat16), 'batch', scatter_...  52.3 us
    reduce_scatter x1, waiting for transfers between devices, body(): lax.psum_scatter(term_shared_out.astype(jnp.bfloat16), 'batch', scatter_d...  52.1 us
    reduce_scatter x1, waiting for transfers between devices, body(): lax.psum_scatter(term_shared_in.astype(jnp.bfloat16), 'batch', scatter_di...  50.5 us
    ppermute x2, waiting for transfers between devices, ring_gather(): lax.ppermute(going_up, axis, [(d, (d + 1) % ways) for d in range(ways)])  36 us
  transfers between devices with their start and end apart: 15, of which 12 were waited for; matrix products, arithmetic and copies ran while one was open for 4% of the time, Pallas kernels for 0%

profile of v1, /device:TPU:1, one launch (start us, length us, event | category | flops | bytes accessed | tf_op | source)
XLA Modules:
  0.0 1729.2 jit_solution(17913941408150616854)
XLA Ops:
  7.3 0.7 all-gather.6.cloned.1.call-update
  8.0 0.7 all-gather.8.cloned.1.call-update
  8.8 0.7 all-gather.4.cloned.1.call-update
  9.7 0.6 broadcast_add_fusion.1
  10.8 1.0 reshape.273
  11.8 13.0 all-to-all-start.2
  24.8 1.4 collective-permute-start
  26.5 1.0 reshape.265
  27.4 14.7 all-to-all-done.2
  42.1 6.3 all-to-all-start
  48.4 2.8 collective-permute-start.1
  51.2 19.1 %collective-permute-done = bf16[1,512,1024]{2,1,0:T(8,128)(2,1)} collective-permute-done((bf16[1,512,1024]{2,1,0:T(8,128)(2,1)S(1)}, bf16[1,512,1024]{2,1,0:T(8,128)(2,1)}, u32[]{:S(2)}, u32[]{:S(2)}) %collective-permute-start) | collective-permute-done | bytes 1048608 | tf_op jit(solution)/shard_map/ppermute | solution.py:22
  70.3 2.1 collective-permute-start.2
  72.4 2.5 broadcast.97
  74.9 1.1 bitcast_dynamic-update-slice_fusion.3
  76.0 0.9 reshape.274
  76.9 0.9 reshape.266
  77.9 2.3 bitcast_dynamic-update-slice_fusion.2
  80.2 7.2 collective-permute-done.1
  87.3 2.3 bitcast_dynamic-update-slice_fusion.1
  89.6 16.9 collective-permute-done.2
  106.5 2.3 bitcast_dynamic-update-slice_fusion
  108.8 5.0 fusion.4
  113.9 33.2 %all-gather.8.cloned.1.call-done = bf16[1,2048,1024]{2,1,0:T(8,128)(2,1)} async-done(((bf16[1,512,1024]{2,1,0:T(8,128)(2,1)}), bf16[1,2048,1024]{2,1,0:T(8,128)(2,1)}) %all-gather.8.cloned.1.call-update) | async-done | bytes 4194320 | tf_op jit(solution)/shard_map/all_gather | solution.py:121
  147.1 4.1 fusion.19
  151.2 0.8 copy.69
  152.0 0.5 broadcast.113
  152.5 3.7 reduce
  156.2 1.1 reshape.283
  157.4 10.9 all-to-all-start.3
  168.3 31.8 %all-gather.4.cloned.1.call-done = bf16[1,1024,2048]{2,1,0:T(8,128)(2,1)} async-done(((bf16[1,1024,512]{2,1,0:T(8,128)(2,1)}), bf16[1,1024,2048]{2,1,0:T(8,128)(2,1)}) %all-gather.4.cloned.1.call-update) | async-done | bytes 4194320 | tf_op jit(solution)/shard_map/all_gather | solution.py:118
  200.1 3.4 fusion.6
  203.5 4.3 fusion.18
  207.8 0.8 copy.70
  208.6 3.7 reduce.1
  212.3 1.1 reshape.285
  213.5 10.7 all-to-all-start.1
  224.2 0.7 pad_add_fusion
  224.9 0.5 fusion.75
  225.6 0.5 reshape.284
  226.1 0.3 fusion.28
  226.5 0.3 fusion.30
  226.8 14.7 all-to-all-done.1
  241.5 0.5 reshape.286
  242.0 0.3 fusion.32
  242.4 1.2 fusion.24
  243.7 1.1 fusion.76
  244.8 3.5 copy.46
  248.6 0.6 copy-done.7
  249.3 0.6 convolution_convert_fusion.1
  250.0 24.2 %all_to_all.24 = bf16[64,4,1024]{2,1,0:T(4,128)(2,1)S(1)} all-to-all(bf16[64,4,1024]{2,1,0:T(4,128)(2,1)S(1)} %reshape.278), channel_id=1, replica_groups=mesh['batch'=4,'expert'=64] {'expert'}, dimensions={0} | all-to-all | bytes 1048576 | tf_op jit(solution)/shard_map/all_to_all | solution.py:153
  274.3 7.4 convert_bitcast_fusion.3
  281.8 4.9 convert_bitcast_fusion.2
  286.9 0.6 convolution_convert_fusion
  287.6 23.2 %all_to_all.25 = bf16[64,4,1024]{2,1,0:T(4,128)(2,1)S(1)} all-to-all(bf16[64,4,1024]{2,1,0:T(4,128)(2,1)S(1)} %reshape.280), channel_id=1, replica_groups=mesh['batch'=4,'expert'=64] {'expert'}, dimensions={0} | all-to-all | bytes 1048576 | tf_op jit(solution)/shard_map/all_to_all | solution.py:154
  311.0 7.4 convert_bitcast_fusion.1
  318.4 4.9 convert_bitcast_fusion
  323.4 1.0 copy-done.3
  324.6 0.9 add_convert_fusion
  325.5 1189.3 %reduce-scatter.14.cloned.1.call-done = f32[4,8,72]{2,1,0:T(8,128)} async-done(((f32[1024,8,72]{2,1,0:T(8,128)}), f32[4,8,72]{2,1,0:T(8,128)}) %reduce-scatter.14.cloned.1.call-update) | async-done | bytes 9232 | tf_op jit(solution)/shard_map/reduce_scatter | solution.py:151
  1514.7 50.5 %reduce-scatter.6.cloned.1.call-done = bf16[1,1024,512]{2,1,0:T(8,128)(2,1)} async-done(((bf16[1,1024,2048]{2,1,0:T(8,128)(2,1)}), bf16[1,1024,512]{2,1,0:T(8,128)(2,1)}) %reduce-scatter.6.cloned.1.call-update) | async-done | bytes 1048592 | tf_op jit(solution)/shard_map/reduce_scatter | solution.py:171
  1565.3 52.1 %reduce-scatter.8.cloned.1.call-done = bf16[1,512,1024]{2,1,0:T(8,128)(2,1)} async-done(((bf16[1,2048,1024]{2,1,0:T(8,128)(2,1)}), bf16[1,512,1024]{2,1,0:T(8,128)(2,1)}) %reduce-scatter.8.cloned.1.call-update) | async-done | bytes 1048592 | tf_op jit(solution)/shard_map/reduce_scatter | solution.py:174
  1617.4 52.4 %reduce-scatter.10.cloned.1.call-done = bf16[1,1024,512]{2,1,0:T(8,128)(2,1)} async-done(((bf16[1,1024,2048]{2,1,0:T(8,128)(2,1)}), bf16[1,1024,512]{2,1,0:T(8,128)(2,1)}) %reduce-scatter.10.cloned.1.call-update) | async-done | bytes 1048592 | tf_op jit(solution)/shard_map/reduce_scatter | solution.py:177
  1669.9 52.3 %reduce-scatter.12.cloned.1.call-done = bf16[1,512,1024]{2,1,0:T(8,128)(2,1)} async-done(((bf16[1,2048,1024]{2,1,0:T(8,128)(2,1)}), bf16[1,512,1024]{2,1,0:T(8,128)(2,1)}) %reduce-scatter.12.cloned.1.call-update) | async-done | bytes 1048592 | tf_op jit(solution)/shard_map/reduce_scatter | solution.py:180
  (73 shorter events, 2.8 us)
Async XLA Ops:
  7.2 217.8 %copy-start = (bf16[1024,8,72]{0,2,1:T(8,128)(2,1)S(1)}, bf16[1024,8,72]{0,2,1:T(8,128)(2,1)}, u32[]{:S(2)}) copy-start(bf16[1024,8,72]{0,2,1:T(8,128)(2,1)} %param.15) | copy-start | bytes 3538948
  7.2 2.3 copy-start.14
  7.2 2.5 copy-start.16
  7.2 2.5 copy-start.15
  7.2 3.3 copy-start.4
  7.2 101.6 %all-gather.6.cloned.1.call-start = ((), (), s32[]{:S(2)}) async-start(), calls=%async_computation.12 | async-start | bytes 5242880 | tf_op jit(solution)/shard_map/all_gather | solution.py:120
  8.0 139.1 %all-gather.8.cloned.1.call-start = ((), (), s32[]{:S(2)}) async-start(), calls=%async_computation.13 | async-start | bytes 5242880 | tf_op jit(solution)/shard_map/all_gather | solution.py:121
  8.7 16.1 copy-start.9
  8.7 191.4 %all-gather.4.cloned.1.call-start = ((), (), s32[]{:S(2)}) async-start(), calls=%async_computation.11 | async-start | bytes 5242880 | tf_op jit(solution)/shard_map/all_gather | solution.py:118
  11.8 30.3 %all-to-all-start.2 = ((bf16[64,4,1024]{2,1,0:T(4,128)(2,1)}), bf16[64,4,1024]{2,1,0:T(4,128)(2,1)S(1)}, u32[]{:S(2)}, u32[]{:S(2)}) async-start(bf16[64,4,1024]{2,1,0:T(4,128)(2,1)} %reshape.273), calls=%async_computation.2 | async-start | bytes 1048576 | tf_op jit(solution)/shard_map/all_to_all | solution.py:115
  24.8 45.6 %collective-permute-start = (bf16[1,512,1024]{2,1,0:T(8,128)(2,1)S(1)}, bf16[1,512,1024]{2,1,0:T(8,128)(2,1)}, u32[]{:S(2)}, u32[]{:S(2)}) collective-permute-start(bf16[1,512,1024]{2,1,0:T(8,128)(2,1)S(1)} %copy-done.9), channel_id=1, source_target_pairs={{0,64},{64,128},{128,192},{192,0},{1,65},{65,129},{129,193},{193,1... | collective-permute-start | bytes 3145736 | tf_op jit(solution)/shard_map/ppermute | solution.py:22
  42.1 34.8 %all-to-all-start = ((bf16[64,4,1024]{2,1,0:T(4,128)(2,1)}), bf16[64,4,1024]{2,1,0:T(4,128)(2,1)S(1)}, u32[]{:S(2)}, u32[]{:S(2)}) async-start(bf16[64,4,1024]{2,1,0:T(4,128)(2,1)} %reshape.265), calls=%async_computation | async-start | bytes 1048576 | tf_op jit(solution)/shard_map/all_to_all | solution.py:114
  48.4 38.9 %collective-permute-start.1 = (bf16[1,512,1024]{2,1,0:T(8,128)(2,1)S(1)}, bf16[1,512,1024]{2,1,0:T(8,128)(2,1)}, u32[]{:S(2)}, u32[]{:S(2)}) collective-permute-start(bf16[1,512,1024]{2,1,0:T(8,128)(2,1)S(1)} %copy-done.9), channel_id=1, source_target_pairs={{0,192},{64,0},{128,64},{192,128},{1,193},{65,1},{129,65},{193,129... | collective-permute-start | bytes 3145736 | tf_op jit(solution)/shard_map/ppermute | solution.py:25
  70.3 36.1 %collective-permute-start.2 = (bf16[1,512,1024]{2,1,0:T(8,128)(2,1)}, bf16[1,512,1024]{2,1,0:T(8,128)(2,1)}, u32[]{:S(2)}, u32[]{:S(2)}) collective-permute-start(bf16[1,512,1024]{2,1,0:T(8,128)(2,1)} %collective-permute-done), channel_id=1, source_target_pairs={{0,64},{64,128},{128,192},{192,0},{1,65},{65,129},{129,193},{193,1... | collective-permute-start | bytes 3145736 | tf_op jit(solution)/shard_map/ppermute | solution.py:22
  80.1 28.7 %copy-start.10 = (bf16[256,1024]{1,0:T(8,128)(2,1)S(1)}, bf16[256,1024]{1,0:T(8,128)(2,1)}, u32[]{:S(2)}) copy-start(bf16[256,1024]{1,0:T(8,128)(2,1)} %reshape.274) | copy-start | bytes 1572868
  152.0 48.1 %copy-start.12 = (bf16[256,1024]{1,0:T(8,128)(2,1)S(1)}, bf16[256,1024]{1,0:T(8,128)(2,1)}, u32[]{:S(2)}) copy-start(bf16[256,1024]{1,0:T(8,128)(2,1)} %reshape.266) | copy-start | bytes 1572868
  157.4 56.1 %all-to-all-start.3 = ((bf16[64,2,2048]{2,1,0:T(2,128)(2,1)}), bf16[64,2,2048]{2,1,0:T(2,128)(2,1)S(1)}, u32[]{:S(2)}, u32[]{:S(2)}) async-start(bf16[64,2,2048]{2,1,0:T(2,128)(2,1)} %reshape.283), calls=%async_computation.3 | async-start | bytes 1048576 | tf_op jit(solution)/shard_map/all_to_all | solution.py:133
  203.5 4.3 copy-start.17
  213.5 28.0 %all-to-all-start.1 = ((bf16[64,2,2048]{2,1,0:T(2,128)(2,1)}), bf16[64,2,2048]{2,1,0:T(2,128)(2,1)S(1)}, u32[]{:S(2)}, u32[]{:S(2)}) async-start(bf16[64,2,2048]{2,1,0:T(2,128)(2,1)} %reshape.285), calls=%async_computation.1 | async-start | bytes 1048576 | tf_op jit(solution)/shard_map/all_to_all | solution.py:130
  224.2 1290.6 %reduce-scatter.14.cloned.1.call-start = ((), (), s32[]{:S(2)}) async-start(), calls=%async_computation.18 | async-start | bytes 4210688 | tf_op jit(solution)/shard_map/reduce_scatter | solution.py:151
  226.5 15.9 copy-start.6
  242.0 1.7 copy-start.5
  242.4 2.5 copy-start.2
  248.3 0.9 copy-start.7
  248.4 26.0 %copy-start.13 = (bf16[256,1024]{1,0:T(8,128)(2,1)S(1)}, bf16[256,1024]{1,0:T(8,128)(2,1)}, u32[]{:S(2)}) copy-start(bf16[256,1024]{1,0:T(8,128)(2,1)} %reshape.266) | copy-start | bytes 1572868
  248.4 1316.9 %reduce-scatter.6.cloned.1.call-start = ((), (), s32[]{:S(2)}) async-start(), calls=%async_computation.14 | async-start | bytes 5242880 | tf_op jit(solution)/shard_map/reduce_scatter | solution.py:171
  281.8 1335.6 %reduce-scatter.8.cloned.1.call-start = ((), (), s32[]{:S(2)}) async-start(), calls=%async_computation.15 | async-start | bytes 5242880 | tf_op jit(solution)/shard_map/reduce_scatter | solution.py:174
  286.8 24.1 %copy-start.11 = (bf16[256,1024]{1,0:T(8,128)(2,1)S(1)}, bf16[256,1024]{1,0:T(8,128)(2,1)}, u32[]{:S(2)}) copy-start(bf16[256,1024]{1,0:T(8,128)(2,1)} %reshape.274) | copy-start | bytes 1572868
  286.8 1383.0 %reduce-scatter.10.cloned.1.call-start = ((), (), s32[]{:S(2)}) async-start(), calls=%async_computation.16 | async-start | bytes 5242880 | tf_op jit(solution)/shard_map/reduce_scatter | solution.py:177
  318.4 1403.8 %reduce-scatter.12.cloned.1.call-start = ((), (), s32[]{:S(2)}) async-start(), calls=%async_computation.17 | async-start | bytes 5242880 | tf_op jit(solution)/shard_map/reduce_scatter | solution.py:180
  323.4 1.0 copy-start.3
  323.4 1.2 copy-start.8
  323.4 1398.8 %copy-start.1 = (bf16[1024,8,72]{0,2,1:T(8,128)(2,1)S(1)}, bf16[1024,8,72]{0,2,1:T(8,128)(2,1)}, u32[]{:S(2)}) copy-start(bf16[1024,8,72]{0,2,1:T(8,128)(2,1)} %param.15) | copy-start | bytes 3538948
Sparse Core Ops, SparseCore 0:
  9.9 84.4 all-gather.5
  96.2 50.8 all-gather.7
  148.9 51.1 all-gather.3
  248.5 1266.2 reduce-scatter.13
  1517.9 47.3 reduce-scatter.5
  1568.2 49.1 reduce-scatter.7
  1620.7 49.1 reduce-scatter.9
  1673.0 49.1 reduce-scatter.11
